TPU v7x, 32 devices: a whole 2x2x4 slice. The times are simulated.
32 devices in a mesh: ctx: 8 (over y, x, core), tp: 4 (over z).
Axes of the slice: x: 2, y: 2, z: 4, core: 2. Of those that a mesh axis runs over, the one named last changes fastest.
Arguments:
- query: bfloat16 [1024, 4096], P('ctx', 'tp'), may hold values from -6 to 6
- keys: bfloat16 [1024, 4096], P('ctx', 'tp'), may hold values from -6 to 6
- values: bfloat16 [1024, 4096], P('ctx', 'tp'), may hold values from -6 to 6
- residues: float32 [4096, 16], P('tp'), may hold values from -0.078125 to 0.078125
- rates: float32 [4096, 16], P('tp'), may hold values from 0.00029296876 to 0.05
- skip_gain: float32 [4096], P('tp'), may hold values from -4 to 4
- w_out: bfloat16 [4096, 4096], P('tp', 'ctx'), may hold values from -0.125 to 0.125
Outputs:
- mixed: bfloat16 [1024, 4096], P('ctx', 'tp')
All inputs are finite; a program needn't handle non-finite values.
Results may differ from a plain program's by a relative error of at most 0.019.
Values may be sent and summed in bfloat16 or wider, within the bound.
A program may use at most 64 MiB of HBM per device.

v0:
```python
import functools

import jax
import jax.numpy as jnp
from jax import lax
from jax.experimental import pallas as pl
from jax.experimental.pallas import tpu as pltpu
from jax.sharding import PartitionSpec as P

MESH = pl.DeviceIdType.MESH
LANES = 128
F32 = jnp.float32
BF16 = jnp.bfloat16


def spread_channels(dst, value):
    for j in range(value.shape[1] // LANES):
        dst[:, j, :] = value[:, j * LANES : (j + 1) * LANES]


def gate_in(keys, values):
    return (keys[...].astype(F32) * values[...].astype(F32)).astype(BF16)


def tree_sum(terms):
    terms = list(terms)
    while len(terms) > 1:
        odd = [terms[-1]] if len(terms) % 2 else []
        terms = [terms[i] + terms[i + 1] for i in range(0, len(terms) - 1, 2)] + odd
    return terms[0]


def run_states(x_ref, lam, start, unroll=8):
    order = lam.shape[0]
    decay = [jnp.exp(-lam[m]) for m in range(order)]

    def body(t, state):
        for u in range(unroll):
            token = x_ref[t * unroll + u]
            state = tuple(decay[m] * state[m] + token for m in range(order))
        return state

    return lax.fori_loop(0, x_ref.shape[0] // unroll, body, start)


def run_conv(x_ref, lam, res, start, unroll=4):
    order = lam.shape[0]
    decay = [jnp.exp(-lam[m]) for m in range(order)]

    def body(t, state):
        for u in range(unroll):
            token = x_ref[t * unroll + u]
            state = tuple(decay[m] * state[m] + token for m in range(order))
            x_ref[t * unroll + u] = tree_sum([res[m] * state[m] for m in range(order)])
        return state

    lax.fori_loop(0, x_ref.shape[0] // unroll, body, start)


def add_carry(y_ref, lam, start, unroll=8):
    order = lam.shape[0]
    decay = [jnp.exp(-lam[m]) for m in range(order)]

    def body(t, state):
        for u in range(unroll):
            state = tuple(decay[m] * state[m] for m in range(order))
            y_ref[t * unroll + u] = y_ref[t * unroll + u] + tree_sum(state)
        return state

    lax.fori_loop(0, y_ref.shape[0] // unroll, body, start)


def gate_out(dst, q_ref, k_ref, v_ref, skip_ref, y_ref):
    for j in range(q_ref.shape[1] // LANES):
        cols = pl.ds(j * LANES, LANES)
        gated_in = (k_ref[:, cols].astype(F32) * v_ref[:, cols].astype(F32)).astype(BF16)
        conv = y_ref[:, j, :].astype(BF16).astype(F32)
        total = conv + skip_ref[:, cols] * gated_in.astype(F32)
        dst[:, cols] = (q_ref[:, cols].astype(F32) * total).astype(BF16)


def flip(number, bits):
    for b in range(bits.bit_length()):
        if bits >> b & 1:
            number = number + (1 << b) - 2 * (1 << b) * (number // (1 << b) % 2)
    return number


def fused_kernel(
    n, tp, q_hbm, k_hbm, v_hbm, res_hbm, rate_hbm, skip_hbm, w_hbm, out_ref,
    q_ref, k_ref, v_ref, res_ref, rate_ref, skip_ref, w_ref,
    x_ref, lam, res, s_own, s_in, s_give, s_got, gated, share, cols_in, from_low, from_high,
    load, s_send, s_recv, c_send, c_recv, g_send, g_recv, f_send, h_send, h_recv,
    p_send, p_recv, z_send, low_recv, high_recv,
):
    me = lax.axis_index("ctx")
    row = lax.axis_index("tp")
    core = me % 2
    chip = me // 2
    sib = me + 1 - 2 * core
    chips = n // 2
    per_tp = n // tp
    tok = q_ref.shape[0]
    half = tok // 2
    order = lam.shape[0]
    shape = lam.shape[1:]

    pairs = (
        (k_hbm, k_ref), (v_hbm, v_ref), (rate_hbm, rate_ref), (res_hbm, res_ref),
        (q_hbm, q_ref), (skip_hbm, skip_ref), (w_hbm, w_ref),
    )
    loads = [pltpu.make_async_copy(src, dst, load.at[i]) for i, (src, dst) in enumerate(pairs)]
    for copy in loads:
        copy.start()

    barrier = pltpu.get_barrier_semaphore()
    for d in range(1, n):
        pl.semaphore_signal(barrier, inc=1, device_id={"ctx": (me + d) % n}, device_id_type=MESH)

    @pl.when(row > 0)
    def _():
        pl.semaphore_signal(barrier, inc=1, device_id={"tp": row - 1}, device_id_type=MESH)

    @pl.when(row < tp - 1)
    def _():
        pl.semaphore_signal(barrier, inc=1, device_id={"tp": row + 1}, device_id_type=MESH)

    for copy in loads[:3]:
        copy.wait()
    spread_channels(x_ref, gate_in(k_ref, v_ref).astype(F32))
    spread_channels(lam, rate_ref[...])
    zero = tuple(jnp.zeros(shape, F32) for _ in range(order))
    state = run_states(x_ref, lam, zero)
    for m in range(order):
        s_own[m] = state[m]

    neighbours = jnp.where(row > 0, 1, 0) + jnp.where(row < tp - 1, 1, 0)
    pl.semaphore_wait(barrier, n - 1 + neighbours)

    def over(axis, index, src, dst, send, recv):
        return pltpu.make_async_remote_copy(
            src_ref=src, dst_ref=dst, send_sem=send, recv_sem=recv,
            device_id={axis: index}, device_id_type=MESH,
        )

    def state_copy(d, slot):
        return over("ctx", flip(chip, d) * 2 + core, s_own, s_in.at[slot], s_send.at[d], s_recv.at[slot])

    for d in range(1, chips):
        state_copy(d, chip).start()
    loads[3].wait()
    spread_channels(res, res_ref[...])
    run_conv(x_ref, lam, res, zero)
    for copy in loads[4:]:
        copy.wait()
    for d in range(1, chips):
        state_copy(d, flip(chip, d)).wait_recv()

    def carry_for(target, dst):
        def weight(source):
            steps = (jnp.maximum(target - 1 - source, 0) * tok).astype(F32)
            live = jnp.where(source < target, 1.0, 0.0).astype(F32)
            return steps, live

        weights = [weight(me)] + [weight(flip(chip, d) * 2 + core) for d in range(1, chips)]
        for m in range(order):
            total = jnp.zeros(shape, F32)
            for d in range(chips):
                part = s_own[m] if d == 0 else s_in[flip(chip, d), m]
                total = total + jnp.exp(-lam[m] * weights[d][0]) * weights[d][1] * part
            dst[m] = total

    carry_for(sib, s_give)
    carry_copy = over("ctx", sib, s_give, s_got, c_send, c_recv)
    carry_copy.start()
    carry_for(me, s_in.at[chip])
    carry_copy.wait_recv()
    add_carry(x_ref, lam, tuple(res[m] * (s_in[chip, m] + s_got[m]) for m in range(order)))
    gate_out(gated.at[me], q_ref, k_ref, v_ref, skip_ref, x_ref)

    def same_core(d):
        return flip(chip, d) * 2 + core

    def other_core(d):
        return flip(chip, d) * 2 + 1 - core

    def gated_copy(index, slot, send):
        return over("ctx", index, gated.at[slot], gated.at[slot], send, g_recv.at[slot])

    def half_copy(index, slot, part):
        rows = pl.ds(part * half, half)
        return over(
            "ctx", index, gated.at[slot, rows], gated.at[slot, rows], h_send.at[part], h_recv.at[part]
        )

    def product(i):
        return jnp.dot(gated[i], w_ref[...], preferred_element_type=F32).astype(BF16)

    def back_copy(i, slot):
        return over("ctx", i, share.at[i], cols_in.at[slot], p_send.at[i], p_recv.at[slot])

    def down_copy(k):
        return over("tp", (row + tp - 1) % tp, cols_in.at[k], from_high.at[k], z_send.at[k], high_recv.at[k])

    def up_copy(k):
        return over("tp", (row + 1) % tp, cols_in.at[k], from_low.at[k], z_send.at[k], low_recv.at[k])

    def send_back(i):
        share[i] = product(i)
        back_copy(i, me).start()

    def send_on(k):
        target = k // per_tp

        @pl.when(row > target)
        def _():
            @pl.when(row < tp - 1)
            def _():
                down_copy(k).wait_recv()
                cols_in[k] = (cols_in[k].astype(F32) + from_high[k].astype(F32)).astype(BF16)

            down_copy(k).start()

        @pl.when(row < target)
        def _():
            @pl.when(row > 0)
            def _():
                up_copy(k).wait_recv()
                cols_in[k] = (cols_in[k].astype(F32) + from_low[k].astype(F32)).astype(BF16)

            up_copy(k).start()

    def arrived(k):
        back_copy(k, k).wait_recv()
        send_on(k)

    def take_other(d):
        i = other_core(d)
        gated_copy(sib, i, f_send.at[d]).wait_recv()
        send_back(i)

    gated_copy(same_core(1), me, g_send.at[1]).start()
    gated_copy(same_core(2), me, g_send.at[2]).start()
    gated_copy(sib, me, g_send.at[0]).start()
    cols_in[me] = product(me)
    gated_copy(sib, sib, g_send.at[0]).wait_recv()
    send_back(sib)
    send_on(me)
    for d in (1, 2):
        i = same_core(d)
        gated_copy(i, i, g_send.at[d]).wait_recv()
        half_copy(same_core(3 - d), i, 2 - d).start()
        gated_copy(sib, i, f_send.at[d]).start()
        send_back(i)
    arrived(sib)
    take_other(1)
    take_other(2)
    arrived(same_core(1))
    arrived(same_core(2))
    far = same_core(3)
    half_copy(me, far, 0).wait_recv()
    half_copy(me, far, 1).wait_recv()
    gated_copy(sib, far, f_send.at[3]).start()
    send_back(far)
    arrived(other_core(1))
    take_other(3)
    arrived(other_core(2))
    arrived(far)
    arrived(other_core(3))

    width = w_ref.shape[1]
    for h in range(per_tp):
        k = row * per_tp + h
        cols = pl.ds(h * width, width)

        @pl.when(row == 0)
        def _():
            down_copy(k).wait_recv()
            out_ref[:, cols] = (cols_in[k].astype(F32) + from_high[k].astype(F32)).astype(BF16)

        @pl.when(row == tp - 1)
        def _():
            up_copy(k).wait_recv()
            out_ref[:, cols] = (cols_in[k].astype(F32) + from_low[k].astype(F32)).astype(BF16)

        @pl.when((row > 0) & (row < tp - 1))
        def _():
            down_copy(k).wait_recv()
            up_copy(k).wait_recv()
            both = from_low[k].astype(F32) + from_high[k].astype(F32)
            out_ref[:, cols] = (cols_in[k].astype(F32) + both).astype(BF16)

    carry_copy.wait_send()
    gated_copy(sib, me, g_send.at[0]).wait_send()
    for d in range(1, chips):
        state_copy(d, chip).wait_send()
        gated_copy(sib, same_core(d), f_send.at[d]).wait_send()
    for d in (1, 2):
        gated_copy(same_core(d), me, g_send.at[d]).wait_send()
        half_copy(same_core(3 - d), same_core(d), 2 - d).wait_send()
    for d in range(1, n):
        back_copy((me + d) % n, me).wait_send()
    for k in range(n):
        @pl.when(k // per_tp != row)
        def _():
            down_copy(k).wait_send()


def fused(n, tp, query, keys, values, residues, rates, skip_gain, w_out):
    tok, chans = query.shape
    order = residues.shape[1]
    width = w_out.shape[1]
    per_tp = n // tp
    poles = (order, chans // LANES, LANES)
    dma = pltpu.SemaphoreType.DMA
    vmem = pltpu.VMEM
    blocks = vmem((n, tok, width), BF16)
    return pl.pallas_call(
        functools.partial(fused_kernel, n, tp),
        out_shape=jax.ShapeDtypeStruct((tok, per_tp * width), BF16),
        in_specs=[pl.BlockSpec(memory_space=pltpu.HBM)] * 7,
        out_specs=pl.BlockSpec(memory_space=pltpu.VMEM),
        scratch_shapes=[
            vmem((tok, chans), BF16), vmem((tok, chans), BF16), vmem((tok, chans), BF16),
            vmem((order, chans), F32), vmem((order, chans), F32), vmem((1, chans), F32),
            vmem((chans, width), BF16),
            vmem((tok,) + poles[1:], F32),
            vmem(poles, F32), vmem(poles, F32), vmem(poles, F32),
            vmem((n // 2,) + poles, F32), vmem(poles, F32), vmem(poles, F32),
            vmem((n, tok, chans), BF16),
            blocks, blocks, blocks, blocks,
            dma((7,)), dma((n // 2,)), dma((n // 2,)), dma, dma, dma((3,)), dma((n,)), dma((n // 2,)),
            dma((2,)), dma((2,)), dma((n,)), dma((n,)), dma((n,)), dma((n,)), dma((n,)),
        ],
        compiler_params=pltpu.CompilerParams(
            collective_id=0, has_side_effects=True, vmem_limit_bytes=60 * 2**20
        ),
    )(query, keys, values, residues.T, rates.T, skip_gain[None, :], w_out)


def states_kernel(k_ref, v_ref, rate_ref, s_ref, x_ref, lam):
    spread_channels(x_ref, gate_in(k_ref, v_ref).astype(F32))
    spread_channels(lam, rate_ref[...])
    zero = tuple(jnp.zeros(lam.shape[1:], F32) for _ in range(lam.shape[0]))
    state = run_states(x_ref, lam, zero)
    for m in range(lam.shape[0]):
        s_ref[m] = state[m]


def conv_kernel(q_ref, k_ref, v_ref, res_ref, rate_ref, skip_ref, s_ref, out_ref, x_ref, lam, res):
    spread_channels(x_ref, gate_in(k_ref, v_ref).astype(F32))
    spread_channels(lam, rate_ref[...])
    spread_channels(res, res_ref[...])
    run_conv(x_ref, lam, res, tuple(s_ref[m] for m in range(lam.shape[0])))
    gate_out(out_ref, q_ref, k_ref, v_ref, skip_ref, x_ref)


def gathered(n, query, keys, values, residues, rates, skip_gain, w_out):
    tok, chans = query.shape
    order = residues.shape[1]
    poles = (order, chans // LANES, LANES)
    block = (tok,) + poles[1:]
    vmem = pl.BlockSpec(memory_space=pltpu.VMEM)
    state = pl.pallas_call(
        states_kernel,
        out_shape=jax.ShapeDtypeStruct(poles, F32),
        in_specs=[vmem] * 3,
        out_specs=vmem,
        scratch_shapes=[pltpu.VMEM(block, F32), pltpu.VMEM(poles, F32)],
        compiler_params=pltpu.CompilerParams(vmem_limit_bytes=24 * 2**20),
    )(keys, values, rates.T)
    me = lax.axis_index("ctx")
    lam = rates.T.reshape(poles)
    blocks = lax.all_gather(state, "ctx")
    away = me - 1 - jnp.arange(n, dtype=jnp.int32)
    steps = (jnp.maximum(away, 0) * tok).astype(F32)[:, None, None, None]
    live = (away >= 0)[:, None, None, None]
    carry = jnp.sum(jnp.where(live, jnp.exp(-lam[None] * steps) * blocks, 0.0), axis=0)
    gated = pl.pallas_call(
        conv_kernel,
        out_shape=jax.ShapeDtypeStruct((tok, chans), BF16),
        in_specs=[vmem] * 7,
        out_specs=vmem,
        scratch_shapes=[pltpu.VMEM(block, F32), pltpu.VMEM(poles, F32), pltpu.VMEM(poles, F32)],
        compiler_params=pltpu.CompilerParams(vmem_limit_bytes=24 * 2**20),
    )(query, keys, values, residues.T, rates.T, skip_gain[None, :], carry)
    weights = lax.all_gather(w_out, "ctx", axis=1, tiled=True)
    part = jnp.dot(gated, weights, preferred_element_type=F32).astype(BF16)
    return lax.psum_scatter(part, "tp", scatter_dimension=1, tiled=True)


def solution(mesh):
    n, tp = mesh.shape["ctx"], mesh.shape["tp"]

    def per_device(query, keys, values, residues, rates, skip_gain, w_out):
        args = (query, keys, values, residues, rates, skip_gain, w_out)
        few_tokens = n * query.shape[0] <= tp * query.shape[1]
        even = n == 8 and n % tp == 0 and w_out.shape[1] % LANES == 0
        if few_tokens and even:
            return fused(n, tp, *args)
        return gathered(n, *args)

    placed = (
        P("ctx", "tp"),
        P("ctx", "tp"),
        P("ctx", "tp"),
        P("tp", None),
        P("tp", None),
        P("tp"),
        P("tp", "ctx"),
    )
    return jax.shard_map(
        per_device, mesh=mesh, in_specs=placed, out_specs=P("ctx", "tp"), check_vma=False
    )
```

profile of v0, /device:TPU:6, one launch (start us, length us, event | category | flops | bytes accessed | tf_op | source)
XLA Modules:
  0.0 55.2 jit_solution(6273040058530799425)
XLA Ops:
  0.0 53.6 %shard_map.73 = bf16[128,1024]{1,0:T(8,128)(2,1)} custom-call(bf16[128,1024]{1,0:T(8,128)(2,1)} %q_hbm.1, bf16[128,1024]{1,0:T(8,128)(2,1)} %k_hbm.1, bf16[128,1024]{1,0:T(8,128)(2,1)} %v_hbm.1, f32[16,1024]{1,0:T(8,128)} %bitcast.3, f32[16,1024]{1,0:T(8,128)} %bitcast.4, f32[1,1024]{1,0:T(1,128)} %bitcast.5, bf16[1024,512]{1,0:T(8,128)(2,1)} %w_hbm.1), custom_call_target="tpu_custom_call" | custom-call | tf_op jit(solution)/shard_map/pallas_call | solution.py:318
  53.6 1.7 %copy.9 = bf16[128,1024]{1,0:T(8,128)(2,1)} copy(bf16[128,1024]{1,0:T(8,128)(2,1)} %shard_map.73) | data formatting | bytes 524288
where the time goes:
time: 55.4 us; the launch traced here: 55.2 us
  Pallas kernels  53.6 us (97%)
  local copies, waits for them, and re-layouts  1.67 us (3%)
    pallas_call x1, Pallas kernels, fused(): pl.pallas_call(functools.partial(fused_kernel, n, tp), out_shape=jax.Shap...  53.6 us
    unnamed x1, local copies, waits for them, and re-layouts  1.67 us

commit v1 on v0

--- a/solution.py
+++ b/solution.py
@@ -89,9 +89,9 @@
 def fused_kernel(
     n, tp, q_hbm, k_hbm, v_hbm, res_hbm, rate_hbm, skip_hbm, w_hbm, out_ref,
     q_ref, k_ref, v_ref, res_ref, rate_ref, skip_ref, w_ref,
-    x_ref, lam, res, s_own, s_in, s_give, s_got, gated, share, cols_in, from_low, from_high,
+    x_ref, lam, res, s_own, s_in, s_give, s_got, gated, share, cols_in, sums_in,
     load, s_send, s_recv, c_send, c_recv, g_send, g_recv, f_send, h_send, h_recv,
-    p_send, p_recv, z_send, low_recv, high_recv,
+    p_send, p_recv, z_send, z_recv,
 ):
     me = lax.axis_index("ctx")
     row = lax.axis_index("tp")
@@ -117,13 +117,8 @@
     for d in range(1, n):
         pl.semaphore_signal(barrier, inc=1, device_id={"ctx": (me + d) % n}, device_id_type=MESH)
 
-    @pl.when(row > 0)
-    def _():
-        pl.semaphore_signal(barrier, inc=1, device_id={"tp": row - 1}, device_id_type=MESH)
-
-    @pl.when(row < tp - 1)
-    def _():
-        pl.semaphore_signal(barrier, inc=1, device_id={"tp": row + 1}, device_id_type=MESH)
+    for d in range(1, tp):
+        pl.semaphore_signal(barrier, inc=1, device_id={"tp": (row + d) % tp}, device_id_type=MESH)
 
     for copy in loads[:3]:
         copy.wait()
@@ -134,8 +129,7 @@
     for m in range(order):
         s_own[m] = state[m]
 
-    neighbours = jnp.where(row > 0, 1, 0) + jnp.where(row < tp - 1, 1, 0)
-    pl.semaphore_wait(barrier, n - 1 + neighbours)
+    pl.semaphore_wait(barrier, n - 1 + tp - 1)
 
     def over(axis, index, src, dst, send, recv):
         return pltpu.make_async_remote_copy(
@@ -199,36 +193,20 @@
     def back_copy(i, slot):
         return over("ctx", i, share.at[i], cols_in.at[slot], p_send.at[i], p_recv.at[slot])
 
-    def down_copy(k):
-        return over("tp", (row + tp - 1) % tp, cols_in.at[k], from_high.at[k], z_send.at[k], high_recv.at[k])
-
-    def up_copy(k):
-        return over("tp", (row + 1) % tp, cols_in.at[k], from_low.at[k], z_send.at[k], low_recv.at[k])
+    def sum_copy(k, source):
+        return over(
+            "tp", k // per_tp, cols_in.at[k], sums_in.at[source, k % per_tp],
+            z_send.at[k], z_recv.at[source, k % per_tp],
+        )
 
     def send_back(i):
         share[i] = product(i)
         back_copy(i, me).start()
 
     def send_on(k):
-        target = k // per_tp
-
-        @pl.when(row > target)
+        @pl.when(k // per_tp != row)
         def _():
-            @pl.when(row < tp - 1)
-            def _():
-                down_copy(k).wait_recv()
-                cols_in[k] = (cols_in[k].astype(F32) + from_high[k].astype(F32)).astype(BF16)
-
-            down_copy(k).start()
-
-        @pl.when(row < target)
-        def _():
-            @pl.when(row > 0)
-            def _():
-                up_copy(k).wait_recv()
-                cols_in[k] = (cols_in[k].astype(F32) + from_low[k].astype(F32)).astype(BF16)
-
-            up_copy(k).start()
+            sum_copy(k, row).start()
 
     def arrived(k):
         back_copy(k, k).wait_recv()
@@ -256,39 +234,26 @@
     take_other(1)
     take_other(2)
     arrived(same_core(1))
-    arrived(same_core(2))
     far = same_core(3)
     half_copy(me, far, 0).wait_recv()
     half_copy(me, far, 1).wait_recv()
     gated_copy(sib, far, f_send.at[3]).start()
     send_back(far)
+    arrived(same_core(2))
+    take_other(3)
     arrived(other_core(1))
-    take_other(3)
     arrived(other_core(2))
     arrived(far)
     arrived(other_core(3))
 
     width = w_ref.shape[1]
     for h in range(per_tp):
-        k = row * per_tp + h
-        cols = pl.ds(h * width, width)
-
-        @pl.when(row == 0)
-        def _():
-            down_copy(k).wait_recv()
-            out_ref[:, cols] = (cols_in[k].astype(F32) + from_high[k].astype(F32)).astype(BF16)
-
-        @pl.when(row == tp - 1)
-        def _():
-            up_copy(k).wait_recv()
-            out_ref[:, cols] = (cols_in[k].astype(F32) + from_low[k].astype(F32)).astype(BF16)
-
-        @pl.when((row > 0) & (row < tp - 1))
-        def _():
-            down_copy(k).wait_recv()
-            up_copy(k).wait_recv()
-            both = from_low[k].astype(F32) + from_high[k].astype(F32)
-            out_ref[:, cols] = (cols_in[k].astype(F32) + both).astype(BF16)
+        total = cols_in[row * per_tp + h].astype(F32)
+        for d in range(1, tp):
+            source = (row + d) % tp
+            sum_copy(row * per_tp + h, source).wait_recv()
+            total = total + sums_in[source, h].astype(F32)
+        out_ref[:, pl.ds(h * width, width)] = total.astype(BF16)
 
     carry_copy.wait_send()
     gated_copy(sib, me, g_send.at[0]).wait_send()
@@ -303,7 +268,7 @@
     for k in range(n):
         @pl.when(k // per_tp != row)
         def _():
-            down_copy(k).wait_send()
+            sum_copy(k, row).wait_send()
 
 
 def fused(n, tp, query, keys, values, residues, rates, skip_gain, w_out):
@@ -328,9 +293,9 @@
             vmem(poles, F32), vmem(poles, F32), vmem(poles, F32),
             vmem((n // 2,) + poles, F32), vmem(poles, F32), vmem(poles, F32),
             vmem((n, tok, chans), BF16),
-            blocks, blocks, blocks, blocks,
+            blocks, blocks, vmem((tp, per_tp, tok, width), BF16),
             dma((7,)), dma((n // 2,)), dma((n // 2,)), dma, dma, dma((3,)), dma((n,)), dma((n // 2,)),
-            dma((2,)), dma((2,)), dma((n,)), dma((n,)), dma((n,)), dma((n,)), dma((n,)),
+            dma((2,)), dma((2,)), dma((n,)), dma((n,)), dma((n,)), dma((tp, per_tp)),
         ],
         compiler_params=pltpu.CompilerParams(
             collective_id=0, has_side_effects=True, vmem_limit_bytes=60 * 2**20

time: 55.4 us -> 54 us (0.975)
  Pallas kernels: 53.6 us -> 52.2 us
    pallas_call x1, Pallas kernels: 53.6 us -> 52.2 us  [fused(): pl.pallas_call(functools.partial(fused_kernel, n, tp), out_shape=jax.Shap...]
where the time goes in v1:
time: 54 us; the launch traced here: 53.9 us
  Pallas kernels  52.2 us (97%)
  local copies, waits for them, and re-layouts  1.67 us (3%)
    pallas_call x1, Pallas kernels, fused(): pl.pallas_call(functools.partial(fused_kernel, n, tp), out_shape=jax.Shap...  52.2 us
    unnamed x1, local copies, waits for them, and re-layouts  1.67 us

profile of v1, /device:TPU:6, one launch (start us, length us, event | category | flops | bytes accessed | tf_op | source)
XLA Modules:
  0.0 53.9 jit_solution(18031723249151229370)
XLA Ops:
  0.0 52.2 %shard_map.73 = bf16[128,1024]{1,0:T(8,128)(2,1)} custom-call(bf16[128,1024]{1,0:T(8,128)(2,1)} %q_hbm.1, bf16[128,1024]{1,0:T(8,128)(2,1)} %k_hbm.1, bf16[128,1024]{1,0:T(8,128)(2,1)} %v_hbm.1, f32[16,1024]{1,0:T(8,128)} %bitcast.3, f32[16,1024]{1,0:T(8,128)} %bitcast.4, f32[1,1024]{1,0:T(1,128)} %bitcast.5, bf16[1024,512]{1,0:T(8,128)(2,1)} %w_hbm.1), custom_call_target="tpu_custom_call" | custom-call | tf_op jit(solution)/shard_map/pallas_call | solution.py:283
  52.2 1.7 %copy.9 = bf16[128,1024]{1,0:T(8,128)(2,1)} copy(bf16[128,1024]{1,0:T(8,128)(2,1)} %shard_map.73) | data formatting | bytes 524288

commit v2 on v1

--- a/solution.py
+++ b/solution.py
@@ -89,9 +89,9 @@
 def fused_kernel(
     n, tp, q_hbm, k_hbm, v_hbm, res_hbm, rate_hbm, skip_hbm, w_hbm, out_ref,
     q_ref, k_ref, v_ref, res_ref, rate_ref, skip_ref, w_ref,
-    x_ref, lam, res, s_own, s_in, s_give, s_got, gated, share, cols_in, sums_in,
+    x_ref, lam, res, s_own, s_in, s_give, s_got, gated, share, cols_in, sums_in, from_low, from_high,
     load, s_send, s_recv, c_send, c_recv, g_send, g_recv, f_send, h_send, h_recv,
-    p_send, p_recv, z_send, z_recv,
+    p_send, p_recv, z_send, z_recv, hop_send, low_recv, high_recv,
 ):
     me = lax.axis_index("ctx")
     row = lax.axis_index("tp")
@@ -199,6 +199,20 @@
             z_send.at[k], z_recv.at[source, k % per_tp],
         )
 
+    def low_copy(k, part):
+        rows = pl.ds(part * half, half)
+        return over(
+            "tp", (row + tp - 1) % tp, cols_in.at[k, rows], from_high.at[k, rows],
+            hop_send.at[k, part], high_recv.at[k, part],
+        )
+
+    def high_copy(k, part):
+        rows = pl.ds(part * half, half)
+        return over(
+            "tp", (row + 1) % tp, cols_in.at[k, rows], from_low.at[k, rows],
+            hop_send.at[k, part], low_recv.at[k, part],
+        )
+
     def send_back(i):
         share[i] = product(i)
         back_copy(i, me).start()
@@ -208,9 +222,31 @@
         def _():
             sum_copy(k, row).start()
 
-    def arrived(k):
+    def hop(k):
         back_copy(k, k).wait_recv()
-        send_on(k)
+        target = k // per_tp
+        for part in range(2):
+            rows = pl.ds(part * half, half)
+
+            @pl.when(row > target)
+            def _():
+                @pl.when(row < tp - 1)
+                def _():
+                    low_copy(k, part).wait_recv()
+                    both = cols_in[k, rows].astype(F32) + from_high[k, rows].astype(F32)
+                    cols_in[k, rows] = both.astype(BF16)
+
+                low_copy(k, part).start()
+
+            @pl.when(row < target)
+            def _():
+                @pl.when(row > 0)
+                def _():
+                    high_copy(k, part).wait_recv()
+                    both = cols_in[k, rows].astype(F32) + from_low[k, rows].astype(F32)
+                    cols_in[k, rows] = both.astype(BF16)
+
+                high_copy(k, part).start()
 
     def take_other(d):
         i = other_core(d)
@@ -230,30 +266,57 @@
         half_copy(same_core(3 - d), i, 2 - d).start()
         gated_copy(sib, i, f_send.at[d]).start()
         send_back(i)
-    arrived(sib)
+    back_copy(sib, sib).wait_recv()
+    send_on(sib)
     take_other(1)
     take_other(2)
-    arrived(same_core(1))
     far = same_core(3)
     half_copy(me, far, 0).wait_recv()
     half_copy(me, far, 1).wait_recv()
     gated_copy(sib, far, f_send.at[3]).start()
     send_back(far)
-    arrived(same_core(2))
     take_other(3)
-    arrived(other_core(1))
-    arrived(other_core(2))
-    arrived(far)
-    arrived(other_core(3))
+    for d in range(1, chips):
+        hop(same_core(d))
+        hop(other_core(d))
 
     width = w_ref.shape[1]
     for h in range(per_tp):
-        total = cols_in[row * per_tp + h].astype(F32)
-        for d in range(1, tp):
-            source = (row + d) % tp
-            sum_copy(row * per_tp + h, source).wait_recv()
-            total = total + sums_in[source, h].astype(F32)
-        out_ref[:, pl.ds(h * width, width)] = total.astype(BF16)
+        k = row * per_tp + h
+        cols = pl.ds(h * width, width)
+
+        @pl.when(row == chip)
+        def _():
+            total = cols_in[k].astype(F32)
+            for d in range(1, tp):
+                source = (row + d) % tp
+                sum_copy(k, source).wait_recv()
+                total = total + sums_in[source, h].astype(F32)
+            out_ref[:, cols] = total.astype(BF16)
+
+        @pl.when(row != chip)
+        def _():
+            for part in range(2):
+                rows = pl.ds(part * half, half)
+
+                @pl.when(row == 0)
+                def _():
+                    low_copy(k, part).wait_recv()
+                    both = cols_in[k, rows].astype(F32) + from_high[k, rows].astype(F32)
+                    out_ref[rows, cols] = both.astype(BF16)
+
+                @pl.when(row == tp - 1)
+                def _():
+                    high_copy(k, part).wait_recv()
+                    both = cols_in[k, rows].astype(F32) + from_low[k, rows].astype(F32)
+                    out_ref[rows, cols] = both.astype(BF16)
+
+                @pl.when((row > 0) & (row < tp - 1))
+                def _():
+                    low_copy(k, part).wait_recv()
+                    high_copy(k, part).wait_recv()
+                    both = from_low[k, rows].astype(F32) + from_high[k, rows].astype(F32)
+                    out_ref[rows, cols] = (cols_in[k, rows].astype(F32) + both).astype(BF16)
 
     carry_copy.wait_send()
     gated_copy(sib, me, g_send.at[0]).wait_send()
@@ -266,9 +329,16 @@
     for d in range(1, n):
         back_copy((me + d) % n, me).wait_send()
     for k in range(n):
-        @pl.when(k // per_tp != row)
+        own = k // per_tp == chip
+
+        @pl.when((k // per_tp != row) & own)
         def _():
             sum_copy(k, row).wait_send()
+
+        @pl.when((k // per_tp != row) & jnp.logical_not(own))
+        def _():
+            for part in range(2):
+                low_copy(k, part).wait_send()
 
 
 def fused(n, tp, query, keys, values, residues, rates, skip_gain, w_out):
@@ -293,9 +363,9 @@
             vmem(poles, F32), vmem(poles, F32), vmem(poles, F32),
             vmem((n // 2,) + poles, F32), vmem(poles, F32), vmem(poles, F32),
             vmem((n, tok, chans), BF16),
-            blocks, blocks, vmem((tp, per_tp, tok, width), BF16),
+            blocks, blocks, vmem((tp, per_tp, tok, width), BF16), blocks, blocks,
             dma((7,)), dma((n // 2,)), dma((n // 2,)), dma, dma, dma((3,)), dma((n,)), dma((n // 2,)),
-            dma((2,)), dma((2,)), dma((n,)), dma((n,)), dma((n,)), dma((tp, per_tp)),
+            dma((2,)), dma((2,)), dma((n,)), dma((n,)), dma((n,)), dma((tp, per_tp)), dma((n, 2)), dma((n, 2)), dma((n, 2)),
         ],
         compiler_params=pltpu.CompilerParams(
             collective_id=0, has_side_effects=True, vmem_limit_bytes=60 * 2**20
@@ -360,7 +430,7 @@
     def per_device(query, keys, values, residues, rates, skip_gain, w_out):
         args = (query, keys, values, residues, rates, skip_gain, w_out)
         few_tokens = n * query.shape[0] <= tp * query.shape[1]
-        even = n == 8 and n % tp == 0 and w_out.shape[1] % LANES == 0
+        even = n == 8 and n == 2 * tp and w_out.shape[1] % LANES == 0
         if few_tokens and even:
             return fused(n, tp, *args)
         return gathered(n, *args)

time: 54 us -> 57.4 us (1.063)
  Pallas kernels: 52.2 us -> 55.5 us
    pallas_call x1, Pallas kernels: 52.2 us -> 55.5 us  [fused(): pl.pallas_call(functools.partial(fused_kernel, n, tp), out_shape=jax.Shap...]
where the time goes in v2:
time: 57.4 us; the launch traced here: 57.2 us
  Pallas kernels  55.5 us (97%)
  local copies, waits for them, and re-layouts  1.67 us (3%)
    pallas_call x1, Pallas kernels, fused(): pl.pallas_call(functools.partial(fused_kernel, n, tp), out_shape=jax.Shap...  55.5 us
    unnamed x1, local copies, waits for them, and re-layouts  1.67 us

profile of v2, /device:TPU:6, one launch (start us, length us, event | category | flops | bytes accessed | tf_op | source)
XLA Modules:
  0.0 57.2 jit_solution(7659523643090210931)
XLA Ops:
  0.0 55.5 %shard_map.73 = bf16[128,1024]{1,0:T(8,128)(2,1)} custom-call(bf16[128,1024]{1,0:T(8,128)(2,1)} %q_hbm.1, bf16[128,1024]{1,0:T(8,128)(2,1)} %k_hbm.1, bf16[128,1024]{1,0:T(8,128)(2,1)} %v_hbm.1, f32[16,1024]{1,0:T(8,128)} %bitcast.3, f32[16,1024]{1,0:T(8,128)} %bitcast.4, f32[1,1024]{1,0:T(1,128)} %bitcast.5, bf16[1024,512]{1,0:T(8,128)(2,1)} %w_hbm.1), custom_call_target="tpu_custom_call" | custom-call | tf_op jit(solution)/shard_map/pallas_call | solution.py:353
  55.5 1.7 %copy.9 = bf16[128,1024]{1,0:T(8,128)(2,1)} copy(bf16[128,1024]{1,0:T(8,128)(2,1)} %shard_map.73) | data formatting | bytes 524288

commit v3 on v1

--- a/solution.py
+++ b/solution.py
@@ -102,6 +102,7 @@
     per_tp = n // tp
     tok = q_ref.shape[0]
     half = tok // 2
+    quarter = tok // 4
     order = lam.shape[0]
     shape = lam.shape[1:]
 
@@ -178,97 +179,137 @@
     def other_core(d):
         return flip(chip, d) * 2 + 1 - core
 
-    def gated_copy(index, slot, send):
-        return over("ctx", index, gated.at[slot], gated.at[slot], send, g_recv.at[slot])
-
-    def half_copy(index, slot, part):
-        rows = pl.ds(part * half, half)
+    def part_of(e):
+        return pl.ds(e * half, half)
+
+    def gated_copy(index, slot, e, send):
+        block = gated.at[slot, part_of(e)]
+        return over("ctx", index, block, block, send, g_recv.at[slot, e])
+
+    def first_copy(d, e):
+        return gated_copy(sib if d == 0 else same_core(d), me, e, g_send.at[d, e])
+
+    def forward_copy(d, e):
+        return gated_copy(sib, same_core(d), e, f_send.at[d, e])
+
+    def relay_copy(index, slot, e, part):
+        block = gated.at[slot, pl.ds(e * half + part * quarter, quarter)]
+        return over("ctx", index, block, block, h_send.at[e, part], h_recv.at[e, part])
+
+    def product(i, e):
+        return jnp.dot(gated[i, part_of(e)], w_ref[...], preferred_element_type=F32).astype(BF16)
+
+    def back_copy(i, slot, e):
         return over(
-            "ctx", index, gated.at[slot, rows], gated.at[slot, rows], h_send.at[part], h_recv.at[part]
+            "ctx", i, share.at[i, part_of(e)], cols_in.at[slot, part_of(e)],
+            p_send.at[i, e], p_recv.at[slot, e],
         )
 
-    def product(i):
-        return jnp.dot(gated[i], w_ref[...], preferred_element_type=F32).astype(BF16)
-
-    def back_copy(i, slot):
-        return over("ctx", i, share.at[i], cols_in.at[slot], p_send.at[i], p_recv.at[slot])
-
-    def sum_copy(k, source):
+    def sum_copy(k, source, e):
         return over(
-            "tp", k // per_tp, cols_in.at[k], sums_in.at[source, k % per_tp],
-            z_send.at[k], z_recv.at[source, k % per_tp],
+            "tp", k // per_tp, cols_in.at[k, part_of(e)], sums_in.at[source, k % per_tp, part_of(e)],
+            z_send.at[k, e], z_recv.at[source, k % per_tp, e],
         )
 
-    def send_back(i):
-        share[i] = product(i)
-        back_copy(i, me).start()
-
-    def send_on(k):
+    def send_back(i, e):
+        share[i, part_of(e)] = product(i, e)
+        back_copy(i, me, e).start()
+
+    def send_on(k, e):
         @pl.when(k // per_tp != row)
         def _():
-            sum_copy(k, row).start()
-
-    def arrived(k):
-        back_copy(k, k).wait_recv()
-        send_on(k)
-
-    def take_other(d):
+            sum_copy(k, row, e).start()
+
+    def arrived(k, e):
+        back_copy(k, k, e).wait_recv()
+        send_on(k, e)
+
+    def take_sib(e):
+        gated_copy(sib, sib, e, g_send.at[0, e]).wait_recv()
+        send_back(sib, e)
+
+    def take_same(d, e):
+        i = same_core(d)
+        gated_copy(i, i, e, g_send.at[d, e]).wait_recv()
+        relay_copy(same_core(3 - d), i, e, 2 - d).start()
+        forward_copy(d, e).start()
+        send_back(i, e)
+
+    def take_far(e):
+        i = same_core(3)
+        relay_copy(me, i, e, 0).wait_recv()
+        relay_copy(me, i, e, 1).wait_recv()
+        forward_copy(3, e).start()
+        send_back(i, e)
+
+    def take_other(d, e):
         i = other_core(d)
-        gated_copy(sib, i, f_send.at[d]).wait_recv()
-        send_back(i)
-
-    gated_copy(same_core(1), me, g_send.at[1]).start()
-    gated_copy(same_core(2), me, g_send.at[2]).start()
-    gated_copy(sib, me, g_send.at[0]).start()
-    cols_in[me] = product(me)
-    gated_copy(sib, sib, g_send.at[0]).wait_recv()
-    send_back(sib)
-    send_on(me)
-    for d in (1, 2):
-        i = same_core(d)
-        gated_copy(i, i, g_send.at[d]).wait_recv()
-        half_copy(same_core(3 - d), i, 2 - d).start()
-        gated_copy(sib, i, f_send.at[d]).start()
-        send_back(i)
-    arrived(sib)
-    take_other(1)
-    take_other(2)
-    arrived(same_core(1))
-    far = same_core(3)
-    half_copy(me, far, 0).wait_recv()
-    half_copy(me, far, 1).wait_recv()
-    gated_copy(sib, far, f_send.at[3]).start()
-    send_back(far)
-    arrived(same_core(2))
-    take_other(3)
-    arrived(other_core(1))
-    arrived(other_core(2))
-    arrived(far)
-    arrived(other_core(3))
+        gated_copy(sib, i, e, f_send.at[d, e]).wait_recv()
+        send_back(i, e)
+
+    def send_first(e):
+        first_copy(1, e).start()
+        first_copy(2, e).start()
+        first_copy(0, e).start()
+        cols_in[me, part_of(e)] = product(me, e)
+        send_on(me, e)
+
+    send_first(0)
+    take_sib(0)
+    for d in range(chips - 1):
+        first_copy(d, 0).wait_send()
+    send_first(1)
+    take_same(1, 0)
+    take_same(2, 0)
+    arrived(sib, 0)
+    take_sib(1)
+    take_other(1, 0)
+    take_other(2, 0)
+    take_far(0)
+    arrived(same_core(1), 0)
+    arrived(same_core(2), 0)
+    take_same(1, 1)
+    take_same(2, 1)
+    take_other(3, 0)
+    arrived(other_core(1), 0)
+    arrived(other_core(2), 0)
+    arrived(sib, 1)
+    take_other(1, 1)
+    take_other(2, 1)
+    take_far(1)
+    arrived(same_core(3), 0)
+    arrived(other_core(3), 0)
+    take_other(3, 1)
+    for d in range(1, chips):
+        arrived(same_core(d), 1)
+        arrived(other_core(d), 1)
 
     width = w_ref.shape[1]
-    for h in range(per_tp):
-        total = cols_in[row * per_tp + h].astype(F32)
-        for d in range(1, tp):
-            source = (row + d) % tp
-            sum_copy(row * per_tp + h, source).wait_recv()
-            total = total + sums_in[source, h].astype(F32)
-        out_ref[:, pl.ds(h * width, width)] = total.astype(BF16)
+    for e in range(2):
+        for h in range(per_tp):
+            total = cols_in[row * per_tp + h, part_of(e)].astype(F32)
+            for d in range(1, tp):
+                source = (row + d) % tp
+                sum_copy(row * per_tp + h, source, e).wait_recv()
+                total = total + sums_in[source, h, part_of(e)].astype(F32)
+            out_ref[part_of(e), pl.ds(h * width, width)] = total.astype(BF16)
 
     carry_copy.wait_send()
-    gated_copy(sib, me, g_send.at[0]).wait_send()
     for d in range(1, chips):
         state_copy(d, chip).wait_send()
-        gated_copy(sib, same_core(d), f_send.at[d]).wait_send()
-    for d in (1, 2):
-        gated_copy(same_core(d), me, g_send.at[d]).wait_send()
-        half_copy(same_core(3 - d), same_core(d), 2 - d).wait_send()
-    for d in range(1, n):
-        back_copy((me + d) % n, me).wait_send()
-    for k in range(n):
-        @pl.when(k // per_tp != row)
-        def _():
-            sum_copy(k, row).wait_send()
+    for d in range(chips - 1):
+        first_copy(d, 1).wait_send()
+    for e in range(2):
+        for d in range(1, chips):
+            forward_copy(d, e).wait_send()
+        for d in (1, 2):
+            relay_copy(same_core(3 - d), same_core(d), e, 2 - d).wait_send()
+        for d in range(1, n):
+            back_copy((me + d) % n, me, e).wait_send()
+        for k in range(n):
+            @pl.when(k // per_tp != row)
+            def _():
+                sum_copy(k, row, e).wait_send()
 
 
 def fused(n, tp, query, keys, values, residues, rates, skip_gain, w_out):
@@ -294,8 +335,8 @@
             vmem((n // 2,) + poles, F32), vmem(poles, F32), vmem(poles, F32),
             vmem((n, tok, chans), BF16),
             blocks, blocks, vmem((tp, per_tp, tok, width), BF16),
-            dma((7,)), dma((n // 2,)), dma((n // 2,)), dma, dma, dma((3,)), dma((n,)), dma((n // 2,)),
-            dma((2,)), dma((2,)), dma((n,)), dma((n,)), dma((n,)), dma((tp, per_tp)),
+            dma((7,)), dma((n // 2,)), dma((n // 2,)), dma, dma, dma((3, 2)), dma((n, 2)), dma((n // 2, 2)),
+            dma((2, 2)), dma((2, 2)), dma((n, 2)), dma((n, 2)), dma((n, 2)), dma((tp, per_tp, 2)),
         ],
         compiler_params=pltpu.CompilerParams(
             collective_id=0, has_side_effects=True, vmem_limit_bytes=60 * 2**20
@@ -360,7 +401,7 @@
     def per_device(query, keys, values, residues, rates, skip_gain, w_out):
         args = (query, keys, values, residues, rates, skip_gain, w_out)
         few_tokens = n * query.shape[0] <= tp * query.shape[1]
-        even = n == 8 and n % tp == 0 and w_out.shape[1] % LANES == 0
+        even = n == 8 and n % tp == 0 and w_out.shape[1] % LANES == 0 and query.shape[0] % 64 == 0
         if few_tokens and even:
             return fused(n, tp, *args)
         return gathered(n, *args)

time: 54 us -> 51.1 us (0.946)
  Pallas kernels: 52.2 us -> 49.3 us
    pallas_call x1, Pallas kernels: 52.2 us -> 49.3 us  [fused(): pl.pallas_call(functools.partial(fused_kernel, n, tp), out_shape=jax.Shap...]
where the time goes in v3:
time: 51.1 us; the launch traced here: 51 us
  Pallas kernels  49.3 us (96%)
  local copies, waits for them, and re-layouts  1.67 us (3%)
    pallas_call x1, Pallas kernels, fused(): pl.pallas_call(functools.partial(fused_kernel, n, tp), out_shape=jax.Shap...  49.3 us
    unnamed x1, local copies, waits for them, and re-layouts  1.67 us

profile of v3, /device:TPU:6, one launch (start us, length us, event | category | flops | bytes accessed | tf_op | source)
XLA Modules:
  0.0 51.0 jit_solution(2905507647303841413)
XLA Ops:
  0.0 49.3 %shard_map.73 = bf16[128,1024]{1,0:T(8,128)(2,1)} custom-call(bf16[128,1024]{1,0:T(8,128)(2,1)} %q_hbm.1, bf16[128,1024]{1,0:T(8,128)(2,1)} %k_hbm.1, bf16[128,1024]{1,0:T(8,128)(2,1)} %v_hbm.1, f32[16,1024]{1,0:T(8,128)} %bitcast.3, f32[16,1024]{1,0:T(8,128)} %bitcast.4, f32[1,1024]{1,0:T(1,128)} %bitcast.5, bf16[1024,512]{1,0:T(8,128)(2,1)} %w_hbm.1), custom_call_target="tpu_custom_call" | custom-call | tf_op jit(solution)/shard_map/pallas_call | solution.py:324
  49.3 1.7 %copy.9 = bf16[128,1024]{1,0:T(8,128)(2,1)} copy(bf16[128,1024]{1,0:T(8,128)(2,1)} %shard_map.73) | data formatting | bytes 524288

commit v4 on v3

--- a/solution.py
+++ b/solution.py
@@ -89,9 +89,9 @@
 def fused_kernel(
     n, tp, q_hbm, k_hbm, v_hbm, res_hbm, rate_hbm, skip_hbm, w_hbm, out_ref,
     q_ref, k_ref, v_ref, res_ref, rate_ref, skip_ref, w_ref,
-    x_ref, lam, res, s_own, s_in, s_give, s_got, gated, share, cols_in, sums_in,
+    x_ref, lam, res, s_own, s_in, s_give, s_got, gated, share, cols_in, sums_in, from_low, from_high,
     load, s_send, s_recv, c_send, c_recv, g_send, g_recv, f_send, h_send, h_recv,
-    p_send, p_recv, z_send, z_recv,
+    p_send, p_recv, z_send, z_recv, hop_send, low_recv, high_recv,
 ):
     me = lax.axis_index("ctx")
     row = lax.axis_index("tp")
@@ -210,6 +210,43 @@
             "tp", k // per_tp, cols_in.at[k, part_of(e)], sums_in.at[source, k % per_tp, part_of(e)],
             z_send.at[k, e], z_recv.at[source, k % per_tp, e],
         )
+
+    def low_copy(k, e):
+        return over(
+            "tp", (row + tp - 1) % tp, cols_in.at[k, part_of(e)], from_high.at[k % per_tp, part_of(e)],
+            hop_send.at[k % per_tp, e], high_recv.at[k % per_tp, e],
+        )
+
+    def high_copy(k, e):
+        return over(
+            "tp", (row + 1) % tp, cols_in.at[k, part_of(e)], from_low.at[k % per_tp, part_of(e)],
+            hop_send.at[k % per_tp, e], low_recv.at[k % per_tp, e],
+        )
+
+    def both(k, e, arrival):
+        return cols_in[k, part_of(e)].astype(F32) + arrival[k % per_tp, part_of(e)].astype(F32)
+
+    def hop(k, e):
+        back_copy(k, k, e).wait_recv()
+        target = k // per_tp
+
+        @pl.when(row > target)
+        def _():
+            @pl.when(row < tp - 1)
+            def _():
+                low_copy(k, e).wait_recv()
+                cols_in[k, part_of(e)] = both(k, e, from_high).astype(BF16)
+
+            low_copy(k, e).start()
+
+        @pl.when(row < target)
+        def _():
+            @pl.when(row > 0)
+            def _():
+                high_copy(k, e).wait_recv()
+                cols_in[k, part_of(e)] = both(k, e, from_low).astype(BF16)
+
+            high_copy(k, e).start()
 
     def send_back(i, e):
         share[i, part_of(e)] = product(i, e)
@@ -277,22 +314,46 @@
     take_other(1, 1)
     take_other(2, 1)
     take_far(1)
-    arrived(same_core(3), 0)
-    arrived(other_core(3), 0)
     take_other(3, 1)
-    for d in range(1, chips):
+    for d in (1, 2):
         arrived(same_core(d), 1)
         arrived(other_core(d), 1)
+    for e in range(2):
+        hop(same_core(3), e)
+        hop(other_core(3), e)
 
     width = w_ref.shape[1]
+    last = flip(chip, 3)
     for e in range(2):
         for h in range(per_tp):
-            total = cols_in[row * per_tp + h, part_of(e)].astype(F32)
-            for d in range(1, tp):
-                source = (row + d) % tp
-                sum_copy(row * per_tp + h, source, e).wait_recv()
-                total = total + sums_in[source, h, part_of(e)].astype(F32)
-            out_ref[part_of(e), pl.ds(h * width, width)] = total.astype(BF16)
+            k = row * per_tp + h
+            cols = pl.ds(h * width, width)
+
+            @pl.when(row != last)
+            def _():
+                total = cols_in[k, part_of(e)].astype(F32)
+                for d in range(1, tp):
+                    source = (row + d) % tp
+                    sum_copy(k, source, e).wait_recv()
+                    total = total + sums_in[source, h, part_of(e)].astype(F32)
+                out_ref[part_of(e), cols] = total.astype(BF16)
+
+            @pl.when((row == last) & (row == 0))
+            def _():
+                low_copy(k, e).wait_recv()
+                out_ref[part_of(e), cols] = both(k, e, from_high).astype(BF16)
+
+            @pl.when((row == last) & (row == tp - 1))
+            def _():
+                high_copy(k, e).wait_recv()
+                out_ref[part_of(e), cols] = both(k, e, from_low).astype(BF16)
+
+            @pl.when((row == last) & (row > 0) & (row < tp - 1))
+            def _():
+                low_copy(k, e).wait_recv()
+                high_copy(k, e).wait_recv()
+                total = both(k, e, from_low) + from_high[k % per_tp, part_of(e)].astype(F32)
+                out_ref[part_of(e), cols] = total.astype(BF16)
 
     carry_copy.wait_send()
     for d in range(1, chips):
@@ -307,9 +368,13 @@
         for d in range(1, n):
             back_copy((me + d) % n, me, e).wait_send()
         for k in range(n):
-            @pl.when(k // per_tp != row)
+            @pl.when((k // per_tp != row) & (k // per_tp != last))
             def _():
                 sum_copy(k, row, e).wait_send()
+
+            @pl.when((k // per_tp != row) & (k // per_tp == last))
+            def _():
+                low_copy(k, e).wait_send()
 
 
 def fused(n, tp, query, keys, values, residues, rates, skip_gain, w_out):
@@ -321,6 +386,7 @@
     dma = pltpu.SemaphoreType.DMA
     vmem = pltpu.VMEM
     blocks = vmem((n, tok, width), BF16)
+    hops = vmem((per_tp, tok, width), BF16)
     return pl.pallas_call(
         functools.partial(fused_kernel, n, tp),
         out_shape=jax.ShapeDtypeStruct((tok, per_tp * width), BF16),
@@ -334,9 +400,10 @@
             vmem(poles, F32), vmem(poles, F32), vmem(poles, F32),
             vmem((n // 2,) + poles, F32), vmem(poles, F32), vmem(poles, F32),
             vmem((n, tok, chans), BF16),
-            blocks, blocks, vmem((tp, per_tp, tok, width), BF16),
+            blocks, blocks, vmem((tp, per_tp, tok, width), BF16), hops, hops,
             dma((7,)), dma((n // 2,)), dma((n // 2,)), dma, dma, dma((3, 2)), dma((n, 2)), dma((n // 2, 2)),
             dma((2, 2)), dma((2, 2)), dma((n, 2)), dma((n, 2)), dma((n, 2)), dma((tp, per_tp, 2)),
+            dma((per_tp, 2)), dma((per_tp, 2)), dma((per_tp, 2)),
         ],
         compiler_params=pltpu.CompilerParams(
             collective_id=0, has_side_effects=True, vmem_limit_bytes=60 * 2**20
@@ -401,7 +468,7 @@
     def per_device(query, keys, values, residues, rates, skip_gain, w_out):
         args = (query, keys, values, residues, rates, skip_gain, w_out)
         few_tokens = n * query.shape[0] <= tp * query.shape[1]
-        even = n == 8 and n % tp == 0 and w_out.shape[1] % LANES == 0 and query.shape[0] % 64 == 0
+        even = n == 8 and n == 2 * tp and w_out.shape[1] % LANES == 0 and query.shape[0] % 64 == 0
         if few_tokens and even:
             return fused(n, tp, *args)
         return gathered(n, *args)

time: 51.1 us -> 54.4 us (1.065)
  Pallas kernels: 49.3 us -> 52.6 us
    pallas_call x1, Pallas kernels: 49.3 us -> 52.6 us  [fused(): pl.pallas_call(functools.partial(fused_kernel, n, tp), out_shape=jax.Shap...]
where the time goes in v4:
time: 54.4 us; the launch traced here: 54.3 us
  Pallas kernels  52.6 us (97%)
  local copies, waits for them, and re-layouts  1.67 us (3%)
    pallas_call x1, Pallas kernels, fused(): pl.pallas_call(functools.partial(fused_kernel, n, tp), out_shape=jax.Shap...  52.6 us
    unnamed x1, local copies, waits for them, and re-layouts  1.67 us

profile of v4, /device:TPU:6, one launch (start us, length us, event | category | flops | bytes accessed | tf_op | source)
XLA Modules:
  0.0 54.3 jit_solution(6608278357031632886)
XLA Ops:
  0.0 52.6 %shard_map.73 = bf16[128,1024]{1,0:T(8,128)(2,1)} custom-call(bf16[128,1024]{1,0:T(8,128)(2,1)} %q_hbm.1, bf16[128,1024]{1,0:T(8,128)(2,1)} %k_hbm.1, bf16[128,1024]{1,0:T(8,128)(2,1)} %v_hbm.1, f32[16,1024]{1,0:T(8,128)} %bitcast.3, f32[16,1024]{1,0:T(8,128)} %bitcast.4, f32[1,1024]{1,0:T(1,128)} %bitcast.5, bf16[1024,512]{1,0:T(8,128)(2,1)} %w_hbm.1), custom_call_target="tpu_custom_call" | custom-call | tf_op jit(solution)/shard_map/pallas_call | solution.py:390
  52.6 1.7 %copy.9 = bf16[128,1024]{1,0:T(8,128)(2,1)} copy(bf16[128,1024]{1,0:T(8,128)(2,1)} %shard_map.73) | data formatting | bytes 524288

commit v5 on v3

--- a/solution.py
+++ b/solution.py
@@ -228,24 +228,32 @@
         gated_copy(sib, sib, e, g_send.at[0, e]).wait_recv()
         send_back(sib, e)
 
-    def take_same(d, e):
+    def receive_same(d, e):
         i = same_core(d)
         gated_copy(i, i, e, g_send.at[d, e]).wait_recv()
         relay_copy(same_core(3 - d), i, e, 2 - d).start()
         forward_copy(d, e).start()
-        send_back(i, e)
-
-    def take_far(e):
+
+    def take_same(d, e):
+        receive_same(d, e)
+        send_back(same_core(d), e)
+
+    def receive_far(e):
         i = same_core(3)
         relay_copy(me, i, e, 0).wait_recv()
         relay_copy(me, i, e, 1).wait_recv()
         forward_copy(3, e).start()
-        send_back(i, e)
+
+    def take_far(e):
+        receive_far(e)
+        send_back(same_core(3), e)
+
+    def receive_other(d, e):
+        gated_copy(sib, other_core(d), e, f_send.at[d, e]).wait_recv()
 
     def take_other(d, e):
-        i = other_core(d)
-        gated_copy(sib, i, e, f_send.at[d, e]).wait_recv()
-        send_back(i, e)
+        receive_other(d, e)
+        send_back(other_core(d), e)
 
     def send_first(e):
         first_copy(1, e).start()
@@ -268,21 +276,32 @@
     take_far(0)
     arrived(same_core(1), 0)
     arrived(same_core(2), 0)
-    take_same(1, 1)
-    take_same(2, 1)
+    receive_same(1, 1)
+    receive_same(2, 1)
+    send_back(same_core(1), 1)
     take_other(3, 0)
     arrived(other_core(1), 0)
     arrived(other_core(2), 0)
     arrived(sib, 1)
     take_other(1, 1)
-    take_other(2, 1)
-    take_far(1)
+    receive_far(1)
+    even = row % 2 == 0
+    near_pair = (same_core(2), other_core(2))
+    far_pair = (same_core(3), other_core(3))
+    third = [jnp.where(even, a, b) for a, b in zip(near_pair, far_pair)]
+    fourth = [jnp.where(even, b, a) for a, b in zip(near_pair, far_pair)]
+    send_back(third[0], 1)
     arrived(same_core(3), 0)
+    receive_other(2, 1)
+    receive_other(3, 1)
+    send_back(third[1], 1)
+    send_back(fourth[0], 1)
+    send_back(fourth[1], 1)
     arrived(other_core(3), 0)
-    take_other(3, 1)
-    for d in range(1, chips):
-        arrived(same_core(d), 1)
-        arrived(other_core(d), 1)
+    arrived(same_core(1), 1)
+    arrived(other_core(1), 1)
+    for k in third + fourth:
+        arrived(k, 1)
 
     width = w_ref.shape[1]
     for e in range(2):
@@ -292,7 +311,7 @@
                 source = (row + d) % tp
                 sum_copy(row * per_tp + h, source, e).wait_recv()
                 total = total + sums_in[source, h, part_of(e)].astype(F32)
-            out_ref[part_of(e), pl.ds(h * width, width)] = total.astype(BF16)
+            out_ref[part_of(e), pl.ds(h * width, width)] = total
 
     carry_copy.wait_send()
     for d in range(1, chips):
@@ -323,7 +342,7 @@
     blocks = vmem((n, tok, width), BF16)
     return pl.pallas_call(
         functools.partial(fused_kernel, n, tp),
-        out_shape=jax.ShapeDtypeStruct((tok, per_tp * width), BF16),
+        out_shape=jax.ShapeDtypeStruct((tok, per_tp * width), F32),
         in_specs=[pl.BlockSpec(memory_space=pltpu.HBM)] * 7,
         out_specs=pl.BlockSpec(memory_space=pltpu.VMEM),
         scratch_shapes=[
@@ -341,7 +360,7 @@
         compiler_params=pltpu.CompilerParams(
             collective_id=0, has_side_effects=True, vmem_limit_bytes=60 * 2**20
         ),
-    )(query, keys, values, residues.T, rates.T, skip_gain[None, :], w_out)
+    )(query, keys, values, residues.T, rates.T, skip_gain[None, :], w_out).astype(BF16)
 
 
 def states_kernel(k_ref, v_ref, rate_ref, s_ref, x_ref, lam):

time: 51.1 us -> 50.7 us (level)
  other arithmetic: 0 us -> 1.78 us
  local copies, waits for them, and re-layouts: 1.67 us -> 0 us
  Pallas kernels: 49.3 us -> 48.5 us
    convert_element_type x0 -> x1, other arithmetic: none -> 1.78 us  [fused(): return pl.pallas_call(functools.partial(fused_kernel, n, tp), out_shape=j...]
    unnamed x1 -> x0, local copies, waits for them, and re-layouts: 1.67 us -> none
    pallas_call x1, Pallas kernels: 49.3 us -> 48.5 us  [fused(): pl.pallas_call(functools.partial(fused_kernel, n, tp), out_shape=jax.Shap...]
where the time goes in v5:
time: 50.7 us; the launch traced here: 50.3 us
  Pallas kernels  48.5 us (96%)
  other arithmetic  1.78 us (4%)
    pallas_call x1, Pallas kernels, fused(): pl.pallas_call(functools.partial(fused_kernel, n, tp), out_shape=jax.Shap...  48.5 us
    convert_element_type x1, other arithmetic, fused(): return pl.pallas_call(functools.partial(fused_kernel, n, tp), out_shape=j...  1.78 us

profile of v5, /device:TPU:6, one launch (start us, length us, event | category | flops | bytes accessed | tf_op | source)
XLA Modules:
  0.0 50.3 jit_solution(10135072096963085219)
XLA Ops:
  0.0 48.5 %shard_map.73 = f32[128,1024]{1,0:T(8,128)} custom-call(bf16[128,1024]{1,0:T(8,128)(2,1)} %q_hbm.1, bf16[128,1024]{1,0:T(8,128)(2,1)} %k_hbm.1, bf16[128,1024]{1,0:T(8,128)(2,1)} %v_hbm.1, f32[16,1024]{1,0:T(8,128)} %bitcast.3, f32[16,1024]{1,0:T(8,128)} %bitcast.4, f32[1,1024]{1,0:T(1,128)} %bitcast.5, bf16[1024,512]{1,0:T(8,128)(2,1)} %w_hbm.1), custom_call_target="tpu_custom_call" | custom-call | tf_op jit(solution)/shard_map/pallas_call | solution.py:343
  48.5 1.8 %convert_element_type.3 = bf16[128,1024]{1,0:T(8,128)(2,1)} convert(f32[128,1024]{1,0:T(8,128)} %shard_map.73) | non-fusion elementwise | flops 131072 | bytes 786432 | tf_op jit(solution)/shard_map/convert_element_type | solution.py:363

commit v6 on v5

--- a/solution.py
+++ b/solution.py
@@ -215,6 +215,14 @@
         share[i, part_of(e)] = product(i, e)
         back_copy(i, me, e).start()
 
+    def send_back_pair(i, j, e):
+        rows = jnp.concatenate([gated[i, part_of(e)], gated[j, part_of(e)]], axis=0)
+        result = jnp.dot(rows, w_ref[...], preferred_element_type=F32).astype(BF16)
+        share[i, part_of(e)] = result[:half]
+        back_copy(i, me, e).start()
+        share[j, part_of(e)] = result[half:]
+        back_copy(j, me, e).start()
+
     def send_on(k, e):
         @pl.when(k // per_tp != row)
         def _():
@@ -233,10 +241,6 @@
         gated_copy(i, i, e, g_send.at[d, e]).wait_recv()
         relay_copy(same_core(3 - d), i, e, 2 - d).start()
         forward_copy(d, e).start()
-
-    def take_same(d, e):
-        receive_same(d, e)
-        send_back(same_core(d), e)
 
     def receive_far(e):
         i = same_core(3)
@@ -267,12 +271,14 @@
     for d in range(chips - 1):
         first_copy(d, 0).wait_send()
     send_first(1)
-    take_same(1, 0)
-    take_same(2, 0)
+    receive_same(1, 0)
+    receive_same(2, 0)
+    send_back_pair(same_core(1), same_core(2), 0)
     arrived(sib, 0)
     take_sib(1)
-    take_other(1, 0)
-    take_other(2, 0)
+    receive_other(1, 0)
+    receive_other(2, 0)
+    send_back_pair(other_core(1), other_core(2), 0)
     take_far(0)
     arrived(same_core(1), 0)
     arrived(same_core(2), 0)
@@ -295,8 +301,7 @@
     receive_other(2, 1)
     receive_other(3, 1)
     send_back(third[1], 1)
-    send_back(fourth[0], 1)
-    send_back(fourth[1], 1)
+    send_back_pair(fourth[0], fourth[1], 1)
     arrived(other_core(3), 0)
     arrived(same_core(1), 1)
     arrived(other_core(1), 1)
@@ -311,7 +316,7 @@
                 source = (row + d) % tp
                 sum_copy(row * per_tp + h, source, e).wait_recv()
                 total = total + sums_in[source, h, part_of(e)].astype(F32)
-            out_ref[part_of(e), pl.ds(h * width, width)] = total
+            out_ref[part_of(e), pl.ds(h * width, width)] = total.astype(BF16)
 
     carry_copy.wait_send()
     for d in range(1, chips):
@@ -342,7 +347,7 @@
     blocks = vmem((n, tok, width), BF16)
     return pl.pallas_call(
         functools.partial(fused_kernel, n, tp),
-        out_shape=jax.ShapeDtypeStruct((tok, per_tp * width), F32),
+        out_shape=jax.ShapeDtypeStruct((tok, per_tp * width), BF16),
         in_specs=[pl.BlockSpec(memory_space=pltpu.HBM)] * 7,
         out_specs=pl.BlockSpec(memory_space=pltpu.VMEM),
         scratch_shapes=[
@@ -358,9 +363,9 @@
             dma((2, 2)), dma((2, 2)), dma((n, 2)), dma((n, 2)), dma((n, 2)), dma((tp, per_tp, 2)),
         ],
         compiler_params=pltpu.CompilerParams(
-            collective_id=0, has_side_effects=True, vmem_limit_bytes=60 * 2**20
+            collective_id=0, has_side_effects=True, vmem_limit_bytes=107 * 2**19
         ),
-    )(query, keys, values, residues.T, rates.T, skip_gain[None, :], w_out).astype(BF16)
+    )(query, keys, values, residues.T, rates.T, skip_gain[None, :], w_out)
 
 
 def states_kernel(k_ref, v_ref, rate_ref, s_ref, x_ref, lam):

time: 50.7 us -> 51 us (level)
  local copies, waits for them, and re-layouts: 0 us -> 3.07 us
  other arithmetic: 1.78 us -> 0 us
  Pallas kernels: 48.5 us -> 47.4 us
    unnamed x0 -> x7, local copies, waits for them, and re-layouts: none -> 3.07 us
    convert_element_type x1 -> x0, other arithmetic: 1.78 us -> none  [fused(): return pl.pallas_call(functools.partial(fused_kernel, n, tp), out_shape=j...]
    pallas_call x1, Pallas kernels: 48.5 us -> 47.4 us  [fused(): pl.pallas_call(functools.partial(fused_kernel, n, tp), out_shape=jax.Shap...]
where the time goes in v6:
time: 51 us; the launch traced here: 50.5 us
  Pallas kernels  47.4 us (93%)
  local copies, waits for them, and re-layouts  3.07 us (6%)
    pallas_call x1, Pallas kernels, fused(): pl.pallas_call(functools.partial(fused_kernel, n, tp), out_shape=jax.Shap...  47.4 us
    unnamed x7, local copies, waits for them, and re-layouts  3.07 us

profile of v6, /device:TPU:6, one launch (start us, length us, event | category | flops | bytes accessed | tf_op | source)
XLA Modules:
  0.0 50.5 jit_solution(114096174838889515)
XLA Ops:
  0.0 0.0 copy-start.2
  0.0 0.7 %copy-done.2 = f32[1024]{0:T(1024)S(1)} copy-done((f32[1024]{0:T(1024)S(1)}, f32[1024]{0:T(1024)}, u32[]{:S(2)}) %copy-start.2) | copy-done | bytes 4120
  0.7 0.0 copy-start
  0.7 0.8 %copy-done = f32[1024,16]{0,1:T(8,128)S(1)} copy-done((f32[1024,16]{0,1:T(8,128)S(1)}, f32[1024,16]{0,1:T(8,128)}, u32[]{:S(2)}) %copy-start) | copy-done | bytes 65560
  1.5 0.0 copy-start.1
  1.5 0.8 %copy-done.1 = f32[1024,16]{0,1:T(8,128)S(1)} copy-done((f32[1024,16]{0,1:T(8,128)S(1)}, f32[1024,16]{0,1:T(8,128)}, u32[]{:S(2)}) %copy-start.1) | copy-done | bytes 65560
  2.4 47.4 %shard_map.73 = bf16[128,1024]{1,0:T(8,128)(2,1)S(1)} custom-call(bf16[128,1024]{1,0:T(8,128)(2,1)} %q_hbm.1, bf16[128,1024]{1,0:T(8,128)(2,1)} %k_hbm.1, bf16[128,1024]{1,0:T(8,128)(2,1)} %v_hbm.1, f32[16,1024]{1,0:T(8,128)S(1)} %bitcast.3, f32[16,1024]{1,0:T(8,128)S(1)} %bitcast.4, f32[1,1024]{1,0:T(1,128)S(1)} %bitcast.5, bf16[1024,512]{1,0:T(8,128)(2,1)} %w_hbm.1), custom_call_target="tpu_custom_call" | custom-call | tf_op jit(solution)/shard_map/pallas_call | solution.py:348
  49.8 0.7 %copy.9 = bf16[128,1024]{1,0:T(8,128)(2,1)} copy(bf16[128,1024]{1,0:T(8,128)(2,1)S(1)} %shard_map.73) | data formatting | bytes 524288
Async XLA Ops:
  0.0 0.7 %copy-start.2 = (f32[1024]{0:T(1024)S(1)}, f32[1024]{0:T(1024)}, u32[]{:S(2)}) copy-start(f32[1024]{0:T(1024)} %param.12) | copy-start | bytes 12292
  0.7 0.8 %copy-start = (f32[1024,16]{0,1:T(8,128)S(1)}, f32[1024,16]{0,1:T(8,128)}, u32[]{:S(2)}) copy-start(f32[1024,16]{0,1:T(8,128)} %param.10) | copy-start | bytes 196612
  1.5 0.8 %copy-start.1 = (f32[1024,16]{0,1:T(8,128)S(1)}, f32[1024,16]{0,1:T(8,128)}, u32[]{:S(2)}) copy-start(f32[1024,16]{0,1:T(8,128)} %param.11) | copy-start | bytes 196612

commit v7 on v6

--- a/solution.py
+++ b/solution.py
@@ -363,7 +363,7 @@
             dma((2, 2)), dma((2, 2)), dma((n, 2)), dma((n, 2)), dma((n, 2)), dma((tp, per_tp, 2)),
         ],
         compiler_params=pltpu.CompilerParams(
-            collective_id=0, has_side_effects=True, vmem_limit_bytes=107 * 2**19
+            collective_id=0, has_side_effects=True, vmem_limit_bytes=60 * 2**20
         ),
     )(query, keys, values, residues.T, rates.T, skip_gain[None, :], w_out)
 

time: 51 us -> 50.2 us (0.984)
  local copies, waits for them, and re-layouts: 3.07 us -> 1.67 us
  Pallas kernels: 47.4 us -> 48.1 us
    unnamed x7 -> x1, local copies, waits for them, and re-layouts: 3.07 us -> 1.67 us
    pallas_call x1, Pallas kernels: 47.4 us -> 48.1 us  [fused(): pl.pallas_call(functools.partial(fused_kernel, n, tp), out_shape=jax.Shap...]
where the time goes in v7:
time: 50.2 us; the launch traced here: 49.8 us
  Pallas kernels  48.1 us (96%)
  local copies, waits for them, and re-layouts  1.67 us (3%)
    pallas_call x1, Pallas kernels, fused(): pl.pallas_call(functools.partial(fused_kernel, n, tp), out_shape=jax.Shap...  48.1 us
    unnamed x1, local copies, waits for them, and re-layouts  1.67 us

profile of v7, /device:TPU:6, one launch (start us, length us, event | category | flops | bytes accessed | tf_op | source)
XLA Modules:
  0.0 49.8 jit_solution(8387110021458453621)
XLA Ops:
  0.0 48.1 %shard_map.73 = bf16[128,1024]{1,0:T(8,128)(2,1)} custom-call(bf16[128,1024]{1,0:T(8,128)(2,1)} %q_hbm.1, bf16[128,1024]{1,0:T(8,128)(2,1)} %k_hbm.1, bf16[128,1024]{1,0:T(8,128)(2,1)} %v_hbm.1, f32[16,1024]{1,0:T(8,128)} %bitcast.3, f32[16,1024]{1,0:T(8,128)} %bitcast.4, f32[1,1024]{1,0:T(1,128)} %bitcast.5, bf16[1024,512]{1,0:T(8,128)(2,1)} %w_hbm.1), custom_call_target="tpu_custom_call" | custom-call | tf_op jit(solution)/shard_map/pallas_call | solution.py:348
  48.1 1.7 %copy.9 = bf16[128,1024]{1,0:T(8,128)(2,1)} copy(bf16[128,1024]{1,0:T(8,128)(2,1)} %shard_map.73) | data formatting | bytes 524288
